TPU v7x, 32 devices: a whole 2x2x4 slice. The times are simulated.
32 devices in a mesh: vir: 8 (over z, x), occ: 4 (over y, core).
Axes of the slice: x: 2, y: 2, z: 4, core: 2. Of those that a mesh axis runs over, the one named last changes fastest.
Arguments:
- integrals: bfloat16 [1024, 1024], P(None, 'vir'), as said below
- amplitudes: bfloat16 [1024, 256], P('vir', 'occ'), may hold values from -6 to 6
- labels: int32 [8], replicated, may hold values from 0 to 7
Outputs:
- residual: bfloat16 [1024, 256], P('vir', 'occ')
Inputs may be any that keep to these rules, and one draw needn't show every extreme that they name: integrals is symmetric: integrals[x, y] == integrals[y, x].
All inputs are finite; a program needn't handle non-finite values.
Results may differ from a plain program's by a relative error of at most 0.001.
Values may be sent and summed in bfloat16 or wider, within the bound.
A program may use at most 64 MiB of HBM per device.

v0:
```python
import jax
import jax.numpy as jnp
from jax import lax
from jax.sharding import PartitionSpec as P

OCC_DEV = 4


def per_device(integrals, amplitudes, labels):
    tile_width = integrals.shape[1]
    pair_cols = amplitudes.shape[1]
    occ_count = lax.axis_size("occ")
    device_index = lax.axis_index("vir")
    own_label = labels[device_index]
    same_label = jnp.repeat(labels == own_label, tile_width)
    row_weight = same_label.astype(jnp.float32)
    ladder = lax.psum_scatter(
        jnp.dot(integrals, amplitudes, preferred_element_type=jnp.float32) * row_weight[:, None],
        "vir",
        scatter_dimension=0,
        tiled=True,
    )
    blocks = ladder.reshape(tile_width, OCC_DEV, occ_count, OCC_DEV)
    received = lax.all_to_all(blocks, "occ", split_axis=2, concat_axis=2, tiled=True)
    mirrored = received.transpose(0, 3, 2, 1).reshape(tile_width, pair_cols)
    return (0.5 * (ladder - mirrored)).astype(jnp.bfloat16)


def solution(mesh):
    placed = (P(None, "vir"), P("vir", "occ"), P())
    return jax.shard_map(
        per_device, mesh=mesh, in_specs=placed, out_specs=P("vir", "occ"), check_vma=False
    )
```

profile of v0, /device:TPU:0, one launch (start us, length us, event | category | flops | bytes accessed | tf_op | source)
XLA Modules:
  0.0 90.6 jit_solution(14280199371306726469)
XLA Ops:
  6.5 0.0 copy-start
  6.5 0.0 copy-start.2
  6.5 0.0 reduce-scatter.2.cloned.1.call-start
  6.5 1.3 %dynamic_slice.3 = s32[1]{0:T(128)} dynamic-slice(s32[8]{0:T(128)} %param.5, s32[]{:T(128)S(6)} %select_n.3), dynamic_slice_sizes={1} | dynamic-slice | bytes 12 | tf_op jit(solution)/shard_map/dynamic_slice | solution.py:14
  7.8 0.0 copy-start.3
  7.8 0.7 copy-done.3
  8.5 0.6 compare_convert_fusion
  9.1 0.1 broadcast_bitcast_fusion
  9.2 0.0 copy-done
  9.2 0.0 copy-done.2
  9.2 0.9 convolution_multiply_fusion
  10.1 0.0 reduce-scatter.2.cloned.1.call-update
  10.1 64.9 %reduce-scatter.2.cloned.1.call-done = f32[128,64]{0,1:T(8,128)} async-done(((f32[1024,64]{0,1:T(8,128)}), f32[128,64]{0,1:T(8,128)}) %reduce-scatter.2.cloned.1.call-update) | async-done | bytes 32784 | tf_op jit(solution)/shard_map/reduce_scatter | solution.py:17
  75.1 0.8 copy.5
  75.8 6.5 %all_to_all.5 = f32[128,4,4,4]{0,1,3,2:T(4,128)S(1)} all-to-all(f32[128,4,4,4]{0,1,3,2:T(4,128)S(1)} %copy.5), channel_id=1, replica_groups=mesh['vir'=8,'occ'=4] {'occ'}, dimensions={2} | all-to-all | bytes 65536 | tf_op jit(solution)/shard_map/all_to_all | solution.py:24
  82.3 0.0 copy-start.1
  82.4 0.7 copy-done.1
  83.1 0.6 multiply_convert_fusion
  (1 shorter events, 0.0 us)
Async XLA Ops:
  6.5 2.7 %copy-start = (bf16[1024,128]{1,0:T(8,128)(2,1)S(1)}, bf16[1024,128]{1,0:T(8,128)(2,1)}, u32[]{:S(2)}) copy-start(bf16[1024,128]{1,0:T(8,128)(2,1)} %param.3) | copy-start | bytes 786436
  6.5 2.7 %copy-start.2 = (bf16[128,64]{0,1:T(8,128)(2,1)S(1)}, bf16[128,64]{0,1:T(8,128)(2,1)}, u32[]{:S(2)}) copy-start(bf16[128,64]{0,1:T(8,128)(2,1)} %param.4) | copy-start | bytes 49156
  6.5 68.5 %reduce-scatter.2.cloned.1.call-start = ((), (), s32[]{:S(2)}) async-start(), calls=%async_computation.2 | async-start | bytes 294912 | tf_op jit(solution)/shard_map/reduce_scatter | solution.py:17
  7.8 0.7 copy-start.3
  82.3 0.8 copy-start.1
Sparse Core Ops, SparseCore 0:
  10.7 64.3 reduce-scatter.1
where the time goes:
time: 90.9 us; the launch traced here: 90.6 us
  waiting for transfers between devices  65 us (72%)
  between operations  13.4 us (15%)
  blocking collectives  6.5 us (7%)
  local copies, waits for them, and re-layouts  3.54 us (4%)
  other arithmetic  1.26 us (1%)
    reduce_scatter x1, waiting for transfers between devices, per_device(): lax.psum_scatter(jnp.dot(integrals, amplitudes, preferred_element_type=jn...  64.9 us
    all_to_all x1, blocking collectives, per_device(): lax.all_to_all(blocks, 'occ', split_axis=2, concat_axis=2, tiled=True)  6.5 us
  transfers between devices with their start and end apart: 1, of which 1 were waited for; matrix products, arithmetic and copies ran while one was open for 0% of the time, Pallas kernels for 0%

commit v1 on v0

v1 whole, which is shorter than its diff:
```python
import functools
import math

import jax
import jax.numpy as jnp
from jax import lax
from jax.experimental import pallas as pl
from jax.experimental.pallas import tpu as pltpu
from jax.sharding import PartitionSpec as P

MESH = pl.DeviceIdType.MESH
UNROLL_UP_TO = 64


def repeat(low, high, body):
    if high - low <= UNROLL_UP_TO:
        for step in range(low, high):
            body(step)
    else:
        lax.fori_loop(low, high, lambda step, carry: (body(step), carry)[1], 0)


def kernel(tiles, owners, q, labels_hbm, integrals_hbm, amplitudes_hbm, out_ref,
           gathered, integrals, outgoing, wide, labels, load_sem, send_sem, recv_sem):
    cols, width = amplitudes_hbm.shape
    nocc = q * owners
    piece = q * q
    me, own = lax.axis_index("vir"), lax.axis_index("occ")

    def peer(step):
        return lax.rem(me + step // owners, tiles), lax.rem(own + step % owners, owners)

    barrier = pltpu.get_barrier_semaphore()

    def greet(step):
        pl.semaphore_signal(barrier, inc=1, device_id=peer(step), device_id_type=MESH)

    load_amplitudes = pltpu.make_async_copy(
        amplitudes_hbm, gathered.at[me, pl.ds(0, cols)], load_sem.at[0])
    load_integrals = pltpu.make_async_copy(integrals_hbm, integrals, load_sem.at[1])
    load_labels = pltpu.make_async_copy(labels_hbm, labels, load_sem.at[2])
    load_amplitudes.start()
    load_labels.start()
    load_integrals.start()
    repeat(1, tiles * owners, greet)

    load_amplitudes.wait()
    wide[pl.ds(0, cols)] = gathered[me, pl.ds(0, cols)].astype(jnp.float32)
    for owner in range(owners):
        rows = [wide[pl.ds(first * nocc + owner * q, q)] for first in range(q)]
        for first in range(q):
            wide[pl.ds(cols + owner * piece + first * q, q)] = rows[first]
    outgoing[...] = wide[pl.ds(cols, cols)].astype(jnp.bfloat16)
    gathered[me, pl.ds(cols + own * piece, piece)] = outgoing[pl.ds(own * piece, piece)]

    load_labels.wait()
    load_integrals.wait()

    def mask(tile):
        same = (labels[tile] == labels[me]).astype(jnp.float32)
        weight = jnp.full((width, width), same, jnp.float32).astype(jnp.bfloat16)
        rows = pl.ds(tile * width, width)
        integrals[rows] = integrals[rows] * weight

    repeat(0, tiles, mask)

    pl.semaphore_wait(barrier, tiles * owners - 1)

    def send(step):
        tile, owner = peer(step)
        shift = step // owners

        def share():
            pltpu.make_async_remote_copy(
                src_ref=outgoing.at[pl.ds(owner * piece, piece)],
                dst_ref=gathered.at[me, pl.ds(cols + own * piece, piece)],
                send_sem=send_sem.at[shift], recv_sem=recv_sem.at[me],
                device_id=(tile, owner), device_id_type=MESH).start()

        def block():
            pltpu.make_async_remote_copy(
                src_ref=gathered.at[me, pl.ds(0, cols)],
                dst_ref=gathered.at[me, pl.ds(0, cols)],
                send_sem=send_sem.at[shift], recv_sem=recv_sem.at[me],
                device_id=(tile, owner), device_id_type=MESH).start()
            pltpu.make_async_remote_copy(
                src_ref=outgoing.at[pl.ds(owner * piece, piece)],
                dst_ref=gathered.at[me, pl.ds(cols + own * piece, piece)],
                send_sem=send_sem.at[shift], recv_sem=recv_sem.at[me],
                device_id=(tile, owner), device_id_type=MESH).start()

        if isinstance(step, int):
            block() if step % owners == 0 else share()
        else:
            lax.cond(step % owners == 0, block, share)

    repeat(1, tiles * owners, send)

    def arrived(shift, rows, semaphores, index):
        held = gathered.at[0, pl.ds(0, rows)]
        pltpu.make_async_copy(held, held, semaphores.at[index]).wait()

    def product(tile):
        return jnp.dot(gathered[tile], integrals[pl.ds(pl.multiple_of(tile * width, width), width)],
                       preferred_element_type=jnp.float32)

    arrived(0, cols - piece, recv_sem, me)
    total = product(me)

    def add(shift, total):
        tile = lax.rem(me + shift, tiles)
        arrived(shift, 2 * cols, recv_sem, tile)
        return total + product(tile)

    if tiles <= UNROLL_UP_TO:
        for shift in range(1, tiles):
            total = add(shift, total)
    else:
        total = lax.fori_loop(1, tiles, add, total)

    wide[...] = total
    for first in range(q):
        ladder = wide[pl.ds(first * nocc, nocc)]
        mirrored = wide[pl.ds(cols + first, nocc, stride=q)]
        out_ref[pl.ds(first * nocc, nocc)] = (0.5 * (ladder - mirrored)).astype(jnp.bfloat16)

    arrived(0, cols - piece, send_sem, 0)
    repeat(1, tiles, lambda shift: arrived(shift, 2 * cols, send_sem, shift))


def per_device(integrals, amplitudes, labels):
    width, cols = amplitudes.shape
    tiles, owners = lax.axis_size("vir"), lax.axis_size("occ")
    q = math.isqrt(cols // owners)
    anywhere = pl.BlockSpec(memory_space=pltpu.HBM)
    flipped = pl.pallas_call(
        functools.partial(kernel, tiles, owners, q),
        out_shape=jax.ShapeDtypeStruct((cols, width), jnp.bfloat16),
        in_specs=[anywhere] * 3,
        out_specs=pl.BlockSpec(memory_space=pltpu.VMEM),
        scratch_shapes=[
            pltpu.VMEM((tiles, 2 * cols, width), jnp.bfloat16),
            pltpu.VMEM((tiles * width, width), jnp.bfloat16),
            pltpu.VMEM((cols, width), jnp.bfloat16),
            pltpu.VMEM((2 * cols, width), jnp.float32),
            pltpu.SMEM(labels.shape, jnp.int32),
            pltpu.SemaphoreType.DMA((3,)),
            pltpu.SemaphoreType.DMA((tiles,)),
            pltpu.SemaphoreType.DMA((tiles,)),
        ],
        compiler_params=pltpu.CompilerParams(
            collective_id=0, has_side_effects=True, vmem_limit_bytes=48 << 20),
        cost_estimate=pl.CostEstimate(
            flops=4 * tiles * width * width * cols,
            bytes_accessed=2 * tiles * width * (width + 2 * cols), transcendentals=0),
    )(labels, integrals, amplitudes.T)
    return flipped.T


def solution(mesh):
    placed = (P(None, "vir"), P("vir", "occ"), P())
    return jax.shard_map(
        per_device, mesh=mesh, in_specs=placed, out_specs=P("vir", "occ"), check_vma=False
    )
```

time: 90.9 us -> 16 us (0.18)
  waiting for transfers between devices: 65 us -> 0 us
  between operations: 13.4 us -> 0.01 us
  Pallas kernels: 0 us -> 12.8 us
  blocking collectives: 6.5 us -> 0 us
  other arithmetic: 1.26 us -> 0 us
    reduce_scatter x1 -> x0, waiting for transfers between devices: 64.9 us -> none  [per_device(): lax.psum_scatter(jnp.dot(integrals, amplitudes, preferred_element_type=jn...]
    pallas_call x0 -> x1, Pallas kernels: none -> 12.8 us  [per_device(): pl.pallas_call(functools.partial(kernel, tiles, owners, q), out_shape=jax...]
    all_to_all x1 -> x0, blocking collectives: 6.5 us -> none  [per_device(): lax.all_to_all(blocks, 'occ', split_axis=2, concat_axis=2, tiled=True)]
    unnamed x8 -> x7, local copies, waits for them, and re-layouts: 1.41 us -> 2.93 us
    dynamic_slice x1 -> x0, local copies, waits for them, and re-layouts: 1.28 us -> none  [per_device(): own_label = labels[device_index]]
    convert_element_type x2 -> x0, other arithmetic: 1.26 us -> none  [the longest x1 0.65 us: per_device(): row_weight = same_label.astype(jnp.float32)]
  transfers between devices with their start and end apart: 1 -> 0, of which waited for: 1 -> 0; matrix products, arithmetic and copies ran while one was open for 0% -> 0% of each run, Pallas kernels for 0% -> 0%
where the time goes in v1:
time: 16 us; the launch traced here: 15.7 us
  Pallas kernels  12.8 us (80%)
  local copies, waits for them, and re-layouts  2.93 us (18%)
    pallas_call x1, Pallas kernels, per_device(): pl.pallas_call(functools.partial(kernel, tiles, owners, q), out_shape=jax...  12.8 us
    unnamed x7, local copies, waits for them, and re-layouts  2.93 us

profile of v1, /device:TPU:0, one launch (start us, length us, event | category | flops | bytes accessed | tf_op | source)
XLA Modules:
  0.0 15.7 jit_solution(11591386415287103858)
XLA Ops:
  0.0 0.0 copy-start.2
  0.0 0.7 %copy-done.2 = s32[8]{0:T(128)S(1)} copy-done((s32[8]{0:T(128)S(1)}, s32[8]{0:T(128)}, u32[]{:S(2)}) %copy-start.2) | copy-done | bytes 56
  0.7 0.0 copy-start
  0.7 0.9 %copy-done = bf16[1024,128]{1,0:T(8,128)(2,1)S(1)} copy-done((bf16[1024,128]{1,0:T(8,128)(2,1)S(1)}, bf16[1024,128]{1,0:T(8,128)(2,1)}, u32[]{:S(2)}) %copy-start) | copy-done | bytes 262168
  1.6 0.0 copy-start.1
  1.6 0.7 %copy-done.1 = bf16[128,64]{0,1:T(8,128)(2,1)S(1)} copy-done((bf16[128,64]{0,1:T(8,128)(2,1)S(1)}, bf16[128,64]{0,1:T(8,128)(2,1)}, u32[]{:S(2)}) %copy-start.1) | copy-done | bytes 16408
  2.3 12.8 %shard_map.37 = bf16[64,128]{1,0:T(8,128)(2,1)S(1)} custom-call(s32[8]{0:T(128)S(1)} %copy-done.2, bf16[1024,128]{1,0:T(8,128)(2,1)S(1)} %copy-done, bf16[64,128]{1,0:T(8,128)(2,1)S(1)} %bitcast.3), custom_call_target="tpu_custom_call" | custom-call | flops 33554432 | bytes 524288 | tf_op jit(solution)/shard_map/pallas_call | solution.py:136
  15.1 0.6 %copy.5 = bf16[128,64]{0,1:T(8,128)(2,1)} copy(bf16[128,64]{0,1:T(8,128)(2,1)S(1)} %bitcast.2) | data formatting | bytes 32768
Async XLA Ops:
  0.0 0.7 %copy-start.2 = (s32[8]{0:T(128)S(1)}, s32[8]{0:T(128)}, u32[]{:S(2)}) copy-start(s32[8]{0:T(128)} %labels_hbm.1) | copy-start | bytes 100
  0.7 0.9 %copy-start = (bf16[1024,128]{1,0:T(8,128)(2,1)S(1)}, bf16[1024,128]{1,0:T(8,128)(2,1)}, u32[]{:S(2)}) copy-start(bf16[1024,128]{1,0:T(8,128)(2,1)} %integrals_hbm.1) | copy-start | bytes 786436
  1.6 0.7 %copy-start.1 = (bf16[128,64]{0,1:T(8,128)(2,1)S(1)}, bf16[128,64]{0,1:T(8,128)(2,1)}, u32[]{:S(2)}) copy-start(bf16[128,64]{0,1:T(8,128)(2,1)} %param.4) | copy-start | bytes 49156
